TPU v7x, 32 devices: a whole 2x2x4 slice. The times are simulated.
32 devices in a mesh: fsdp: 4 (over x, core), seq: 8 (over z, y).
Axes of the slice: x: 2, y: 2, z: 4, core: 2. Of those that a mesh axis runs over, the one named last changes fastest.
Arguments:
- qkv: bfloat16 [4, 1024, 6144], P('fsdp', 'seq'), may hold values from -128 to 128
- resid: bfloat16 [4, 1024, 2048], P('fsdp', 'seq'), may hold values from -0.625 to 0.625
- earlier: float32 [4, 1024, 2048], P('fsdp', 'seq'), may hold values from -12 to 12
- lengths: int32 [4, 12], P('fsdp'), may hold values from 1 to 128, 1024 in all within a row
- teacher_out: bfloat16 [2048, 2048], P('seq', 'fsdp'), may hold values from -6 to 6
- student_out: bfloat16 [2048, 2048], P('seq', 'fsdp'), may hold values from -6 to 6
Outputs:
- targets: float32 [4, 1024, 2048], P('fsdp', 'seq')
- teacher_new: bfloat16 [2048, 2048], P('seq', 'fsdp')
Inputs may be any that keep to these rules, and one draw needn't show every extreme that they name: Each pack's 12 utterance lengths add up to its 1024 frames, and one of them is exactly 128.
All inputs are finite; a program needn't handle non-finite values.
Results may differ from a plain program's by a relative error of at most 0.0019.
Values may be sent and summed in bfloat16 or wider, within the bound.
A program may use at most 64 MiB of HBM per device.

v0:
```python
import math

import jax
import jax.numpy as jnp
from jax import lax
from jax.sharding import PartitionSpec as P

D = 2048
HEADS = 32
HEAD_DIM = 64
TOP_K = 8


ema_decay = 0.9
norm_epsilon = 1e-05
masked_score = -1e30


def segment_ids(utt_lengths, frames):
    utt_ends = jnp.cumsum(utt_lengths)
    places = jnp.arange(frames, dtype=jnp.int32)
    return jnp.sum((places[:, None] >= utt_ends[None, :]).astype(jnp.int32), axis=1)


def attend_window(stacked, segment):
    frames = stacked.shape[0]
    longest = frames // 8
    rows_block = min(512, frames)
    key_span = min(frames, rows_block + 2 * longest)
    inverse_root = 1.0 / math.sqrt(stacked.shape[-1])
    queries = stacked[:, 0]
    keys_all = stacked[:, 1]
    values_all = stacked[:, 2]

    def one_block(row_start):
        key_start = jnp.clip(row_start - longest, 0, frames - key_span)
        block_queries = lax.dynamic_slice_in_dim(queries, row_start, rows_block, 0)
        query_segment = lax.dynamic_slice_in_dim(segment, row_start, rows_block, 0)
        block_keys = lax.dynamic_slice_in_dim(keys_all, key_start, key_span, 0)
        block_values = lax.dynamic_slice_in_dim(values_all, key_start, key_span, 0)
        key_segment = lax.dynamic_slice_in_dim(segment, key_start, key_span, 0)
        scores = (
            jnp.einsum(
                "qhd,khd->hqk", block_queries, block_keys, preferred_element_type=jnp.float32
            )
            * inverse_root
        )
        allowed = (query_segment[:, None] == key_segment[None, :])[None]
        scores = jnp.where(allowed, scores, masked_score)
        row_max = jnp.max(scores, axis=2, keepdims=True)
        weights = jnp.exp(scores - row_max)
        row_total = jnp.sum(weights, axis=2)
        summed = jnp.einsum(
            "hqk,khd->qhd",
            weights.astype(jnp.bfloat16),
            block_values,
            preferred_element_type=jnp.float32,
        )
        return (summed / jnp.transpose(row_total)[:, :, None]).astype(jnp.bfloat16)

    starts = jnp.arange(frames // rows_block, dtype=jnp.int32) * rows_block
    outputs = lax.map(one_block, starts)
    return outputs.reshape(frames, stacked.shape[2], stacked.shape[3])


def shards(qkv, resid, earlier, lengths, teacher_out, student_out):
    teacher_new = (
        ema_decay * teacher_out.astype(jnp.float32)
        + (1.0 - ema_decay) * student_out.astype(jnp.float32)
    ).astype(jnp.bfloat16)
    tokens = qkv.shape[1]
    groups = lax.axis_size("seq")
    frames = tokens * groups
    segment = segment_ids(lengths[0], frames)
    own_heads = qkv[0].reshape(tokens, 3, groups, HEADS // groups, HEAD_DIM)
    attended = attend_window(
        lax.all_to_all(own_heads, "seq", split_axis=2, concat_axis=0, tiled=True)[:, :, 0], segment
    )
    regathered = lax.all_to_all(attended[:, None], "seq", split_axis=0, concat_axis=1, tiled=True)
    mixed_rows = regathered.reshape(tokens, D)
    full_rows = lax.all_gather(teacher_new, "seq", axis=0, tiled=True)
    branch = jnp.dot(
        mixed_rows,
        lax.all_gather(full_rows, "fsdp", axis=1, tiled=True),
        preferred_element_type=jnp.float32,
    )
    branch = branch / math.sqrt(D)
    summed = resid[0].astype(jnp.float32) + branch
    centered = summed - jnp.mean(summed, axis=1, keepdims=True)
    normed = centered * lax.rsqrt(
        jnp.mean(centered * centered, axis=1, keepdims=True) + norm_epsilon
    )
    targets = ((earlier[0] + normed) / TOP_K)[None]
    return (targets, teacher_new)


def solution(mesh):
    placed = (
        P("fsdp", "seq", None),
        P("fsdp", "seq", None),
        P("fsdp", "seq", None),
        P("fsdp", None),
        P("seq", "fsdp"),
        P("seq", "fsdp"),
    )
    return jax.shard_map(
        shards,
        mesh=mesh,
        in_specs=placed,
        out_specs=(P("fsdp", "seq", None), P("seq", "fsdp")),
        check_vma=False,
    )
```

profile of v0, /device:TPU:0, one launch (start us, length us, event | category | flops | bytes accessed | tf_op | source)
XLA Modules:
  0.0 165.1 jit_solution(17810026327615569494)
XLA Ops:
  7.2 1.8 %add_convert_fusion = bf16[256,512]{1,0:T(8,128)(2,1)} fusion(bf16[256,512]{1,0:T(8,128)(2,1)} %param.13, bf16[256,512]{1,0:T(8,128)(2,1)} %param.12), kind=kLoop, calls=%fused_computation.30 | loop fusion | flops 786432 | bytes 786432 | tf_op jit(solution)/shard_map/convert_element_type | solution.py:70
  9.1 53.6 %all-gather.3.cloned.1.call-done = bf16[2048,512]{1,0:T(8,128)(2,1)} async-done(((bf16[256,512]{1,0:T(8,128)(2,1)}), bf16[2048,512]{1,0:T(8,128)(2,1)}) %all-gather.3.cloned.1.call-update) | async-done | bytes 2097168 | tf_op jit(solution)/shard_map/all_gather | solution.py:81
  62.8 1.9 %copy.28 = bf16[1,128,6144]{1,2,0:T(8,128)(2,1)S(1)} copy(bf16[1,128,6144]{2,1,0:T(8,128)(2,1)} %param.8) | data formatting | bytes 3145728 | tf_op args[0]
  64.7 1.3 copy.29
  66.0 3.6 %all-to-all-start = ((bf16[128,3,8,4,64]{0,4,3,1,2:T(8,128)(2,1)}), bf16[128,3,8,4,64]{0,4,3,1,2:T(8,128)(2,1)S(1)}, u32[]{:S(2)}, u32[]{:S(2)}) async-start(bf16[128,3,8,4,64]{0,4,3,1,2:T(8,128)(2,1)} %copy.29), calls=%async_computation | async-start | bytes 3145728 | tf_op jit(solution)/shard_map/all_to_all | solution.py:77
  69.9 36.1 %all-to-all-done = bf16[128,3,8,4,64]{0,4,3,1,2:T(8,128)(2,1)S(1)} async-done(((bf16[128,3,8,4,64]{0,4,3,1,2:T(8,128)(2,1)}), bf16[128,3,8,4,64]{0,4,3,1,2:T(8,128)(2,1)S(1)}, u32[]{:S(2)}, u32[]{:S(2)}) %all-to-all-start) | async-done | bytes 1572896 | tf_op jit(solution)/shard_map/all_to_all | solution.py:77
  106.0 2.4 %copy.30 = bf16[8,128,3,1,4,64]{1,0,5,4,2,3:T(8,128)(2,1)} copy(bf16[8,128,3,1,4,64]{1,5,4,2,0,3:T(8,128)(2,1)S(1)} %bitcast.57) | data formatting | bytes 3145728 | tf_op jit(solution)/shard_map/all_to_all | solution.py:77
  108.4 2.5 %squeeze.25 = bf16[1024,3,4,64]{0,3,2,1:T(8,128)(2,1)S(1)} reshape(bf16[8,128,3,1,4,64]{1,0,5,4,2,3:T(8,128)(2,1)} %copy.30) | data formatting | bytes 3145728 | tf_op jit(solution)/shard_map/squeeze | solution.py:77
  111.0 1.0 slice_bitcast_fusion
  111.9 19.0 %while.12 = (s32[]{:T(128)}, bf16[2,512,4,64]{1,3,2,0:T(8,128)(2,1)S(1)}, s32[2]{0:T(128)S(1)}, bf16[1024,4,64]{0,2,1:T(8,128)(2,1)}, s32[1024]{0:T(1024)S(1)}, ...) while((s32[]{:T(128)}, ...), condition=%wide.region_5.6_spmd, body=%wide.region_2.5_spmd.sunk | while | flops 420605952 | bytes 23911676 | solution.py:62
  115.7 1.8 %fusion.42 = (f32[4,512]{1,0:T(4,128)S(1)}, f32[4,512,768]{2,1,0:T(8,128)S(1)}) fusion(pred[512,768]{1,0:T(8,128)(4,1)S(1)} %broadcast_compare_fusion.2, bf16[1024,4,64]{0,2,1:T(8,128)(2,1)S(1)} %get-tuple-element.190, s32[]{:T(128)S(6)} %min.8, bf16[1024,4,64]{0,2,1:T(8,128)(2,1)S(1)} %get-tuple-element.189, s32[]{:T(128)S(6)} %select_n.44), kind=kOutput, calls=%fused_computation.2.clone.1 | convolution fusion | flops 206043136 | bytes 7348232 | tf_op jit(solution)/shard_map/while/body/eval_jaxpr/qhd,khd->hqk/dot_general | solution.py:43
  117.5 1.7 %fusion.43 = f32[4,512]{1,0:T(4,128)S(1)} fusion(f32[4,512,768]{2,1,0:T(8,128)S(1)} %get-tuple-element.158, f32[4,512]{1,0:T(4,128)S(1)} %get-tuple-element.159, pred[512,768]{1,0:T(8,128)(4,1)S(1)} %broadcast_compare_fusion.2), kind=kLoop, calls=%fused_computation.3.clone.1 | loop fusion | flops 6289408 | bytes 6701056 | tf_op jit(solution)/shard_map/while/body/eval_jaxpr/reduce_sum | solution.py:52
  119.2 2.2 %fusion.44 = bf16[2,512,4,64]{1,3,2,0:T(8,128)(2,1)S(1)} fusion(bf16[2,512,4,64]{1,3,2,0:T(8,128)(2,1)S(1)} %get-tuple-element.173, s32[]{:T(128)} %get-tuple-element.172, f32[4,512,768]{2,1,0:T(8,128)S(1)} %get-tuple-element.158, f32[4,512]{1,0:T(4,128)S(1)} %get-tuple-element.159, pred[512,768]{1,0:T(8,128)(4,1)S(1)} %broadcast_compare_fusion.2, ...), kind=kOutput, calls=%fused_computation.11.clone.1 | convolution fusion | flops 207880192 | bytes 7356424 | tf_op jit(solution)/shard_map/while/body/eval_jaxpr/hqk,khd->qhd/dot_general | solution.py:53
  121.4 0.7 dynamic_slice.56
  125.2 1.8 %fusion.42 = (f32[4,512]{1,0:T(4,128)S(1)}, f32[4,512,768]{2,1,0:T(8,128)S(1)}) fusion(pred[512,768]{1,0:T(8,128)(4,1)S(1)} %broadcast_compare_fusion.2, bf16[1024,4,64]{0,2,1:T(8,128)(2,1)S(1)} %get-tuple-element.190, s32[]{:T(128)S(6)} %min.8, bf16[1024,4,64]{0,2,1:T(8,128)(2,1)S(1)} %get-tuple-element.189, s32[]{:T(128)S(6)} %select_n.44), kind=kOutput, calls=%fused_computation.2.clone.1 | convolution fusion | flops 206043136 | bytes 7348232 | tf_op jit(solution)/shard_map/while/body/eval_jaxpr/qhd,khd->hqk/dot_general | solution.py:43
  127.0 1.7 %fusion.43 = f32[4,512]{1,0:T(4,128)S(1)} fusion(f32[4,512,768]{2,1,0:T(8,128)S(1)} %get-tuple-element.158, f32[4,512]{1,0:T(4,128)S(1)} %get-tuple-element.159, pred[512,768]{1,0:T(8,128)(4,1)S(1)} %broadcast_compare_fusion.2), kind=kLoop, calls=%fused_computation.3.clone.1 | loop fusion | flops 6289408 | bytes 6701056 | tf_op jit(solution)/shard_map/while/body/eval_jaxpr/reduce_sum | solution.py:52
  128.7 2.2 %fusion.44 = bf16[2,512,4,64]{1,3,2,0:T(8,128)(2,1)S(1)} fusion(bf16[2,512,4,64]{1,3,2,0:T(8,128)(2,1)S(1)} %get-tuple-element.173, s32[]{:T(128)} %get-tuple-element.172, f32[4,512,768]{2,1,0:T(8,128)S(1)} %get-tuple-element.158, f32[4,512]{1,0:T(4,128)S(1)} %get-tuple-element.159, pred[512,768]{1,0:T(8,128)(4,1)S(1)} %broadcast_compare_fusion.2, ...), kind=kOutput, calls=%fused_computation.11.clone.1 | convolution fusion | flops 207880192 | bytes 7356424 | tf_op jit(solution)/shard_map/while/body/eval_jaxpr/hqk,khd->qhd/dot_general | solution.py:53
  131.0 0.7 copy.35
  131.7 0.7 reshape.80
  132.4 18.1 %all_to_all.30 = bf16[8,2,16384]{2,1,0:T(2,128)(2,1)S(1)} all-to-all(bf16[8,2,16384]{2,1,0:T(2,128)(2,1)S(1)} %reshape.80), channel_id=1, replica_groups=mesh['fsdp'=4,'seq'=8] {'seq'}, dimensions={0} | all-to-all | bytes 1048576 | tf_op jit(solution)/shard_map/all_to_all | solution.py:79
  150.5 0.7 reshape.81
  151.1 0.6 copy.36
  152.0 4.8 %fusion.32 = (f32[128]{0:T(128)S(1)}, f32[128,2048]{1,0:T(8,128)S(1)}) fusion(bf16[128,2048]{0,1:T(8,128)(2,1)S(1)} %bitcast.61, bf16[2048,2048]{1,0:T(8,128)(2,1)} %all-gather.5.cloned.1.call-done, bf16[1,128,2048]{2,1,0:T(8,128)(2,1)S(1)} %copy-done.1), kind=kOutput, calls=%fused_computation.36 | convolution fusion | flops 1074790272 | bytes 10486272 | tf_op jit(solution)/shard_map/dot_general | solution.py:82
  157.1 1.2 fusion.31
  (30 shorter events, 2.4 us)
Async XLA Ops:
  7.2 62.5 %copy-start.3 = (s32[1,12]{1,0:T(1,128)S(1)}, s32[1,12]{1,0:T(1,128)}, u32[]{:S(2)}) copy-start(s32[1,12]{1,0:T(1,128)} %param.11) | copy-start | bytes 148
  7.2 55.6 %all-gather.3.cloned.1.call-start = ((), (), s32[]{:S(2)}) async-start(), calls=%async_computation.2 | async-start | bytes 2359296 | tf_op jit(solution)/shard_map/all_gather | solution.py:81
  9.1 142.9 %all-gather.5.cloned.1.call-start = ((), (), s32[]{:S(2)}) async-start(), calls=%async_computation.3 | async-start | bytes 10485760 | tf_op jit(solution)/shard_map/all_gather | solution.py:84
  66.0 40.0 %all-to-all-start = ((bf16[128,3,8,4,64]{0,4,3,1,2:T(8,128)(2,1)}), bf16[128,3,8,4,64]{0,4,3,1,2:T(8,128)(2,1)S(1)}, u32[]{:S(2)}, u32[]{:S(2)}) async-start(bf16[128,3,8,4,64]{0,4,3,1,2:T(8,128)(2,1)} %copy.29), calls=%async_computation | async-start | bytes 3145728 | tf_op jit(solution)/shard_map/all_to_all | solution.py:77
  115.7 3.5 %copy-start.2 = (bf16[1024,4,64]{0,2,1:T(8,128)(2,1)S(1)}, bf16[1024,4,64]{0,2,1:T(8,128)(2,1)}, u32[]{:S(2)}) copy-start(bf16[1024,4,64]{0,2,1:T(8,128)(2,1)} %get-tuple-element.187) | copy-start | bytes 1572868 | tf_op jit(solution)/shard_map/while
  125.2 3.5 %copy-start.2 = (bf16[1024,4,64]{0,2,1:T(8,128)(2,1)S(1)}, bf16[1024,4,64]{0,2,1:T(8,128)(2,1)}, u32[]{:S(2)}) copy-start(bf16[1024,4,64]{0,2,1:T(8,128)(2,1)} %get-tuple-element.187) | copy-start | bytes 1572868 | tf_op jit(solution)/shard_map/while
  130.9 21.0 %copy-start.1 = (bf16[1,128,2048]{2,1,0:T(8,128)(2,1)S(1)}, bf16[1,128,2048]{2,1,0:T(8,128)(2,1)}, u32[]{:S(2)}) copy-start(bf16[1,128,2048]{2,1,0:T(8,128)(2,1)} %param.9) | copy-start | bytes 1572868
  151.9 5.1 %copy-start = (f32[1,128,2048]{2,1,0:T(8,128)S(1)}, f32[1,128,2048]{2,1,0:T(8,128)}, u32[]{:S(2)}) copy-start(f32[1,128,2048]{2,1,0:T(8,128)} %param.10) | copy-start | bytes 3145732
Sparse Core Ops, SparseCore 0:
  10.7 51.9 all-gather.2
  64.3 56.7 all-gather.4
where the time goes:
time: 166 us; the launch traced here: 165 us
  waiting for transfers between devices  89.8 us (54%)
  blocking collectives  18.1 us (11%)
  between operations  14.2 us (9%)
  local copies, waits for them, and re-layouts  13.6 us (8%)
  matrix products  12.8 us (8%)
  other arithmetic  7.53 us (5%)
  loops' own time  5.47 us (3%)
  starting transfers between devices  3.7 us (2%)
    all_gather x1, waiting for transfers between devices, shards(): full_rows = lax.all_gather(teacher_new, 'seq', axis=0, tiled=True)  53.6 us
    all_to_all x1, waiting for transfers between devices, shards(): lax.all_to_all(own_heads, 'seq', split_axis=2, concat_axis=0, tiled=True)  36.1 us
    all_to_all x1, blocking collectives, shards(): lax.all_to_all(attended[:, None], 'seq', split_axis=0, concat_axis=1, til...  18.1 us
    another operation x1, loops' own time, attend_window(): outputs = lax.map(one_block, starts)  5.47 us
    dot_general x1, matrix products, shards(): jnp.dot(mixed_rows, lax.all_gather(full_rows, 'fsdp', axis=1, tiled=True)...  4.83 us
    dot_general x2, matrix products, one_block(): jnp.einsum('hqk,khd->qhd', weights.astype(jnp.bfloat16), block_values, pr...  4.39 us
    all_to_all x1, starting transfers between devices, shards(): lax.all_to_all(own_heads, 'seq', split_axis=2, concat_axis=0, tiled=True)  3.62 us
    dot_general x2, matrix products, one_block(): jnp.einsum('qhd,khd->hqk', block_queries, block_keys, preferred_element_t...  3.59 us
  transfers between devices with their start and end apart: 3, of which 2 were waited for; matrix products, arithmetic and copies ran while one was open for 16% of the time, Pallas kernels for 0%

commit v1 on v0

--- a/solution.py
+++ b/solution.py
@@ -1,23 +1,326 @@
+import functools
 import math
 
 import jax
 import jax.numpy as jnp
 from jax import lax
+from jax.experimental import pallas as pl
+from jax.experimental.pallas import tpu as pltpu
 from jax.sharding import PartitionSpec as P
 
-D = 2048
 HEADS = 32
 HEAD_DIM = 64
 TOP_K = 8
-
+PAIR = 2
 
 ema_decay = 0.9
 norm_epsilon = 1e-05
 masked_score = -1e30
+log2_e = math.log2(math.e)
+
+
+def body(
+    F, S, H,
+    len_ref, qkv_ref, resid_ref, earlier_ref, tea_ref, stu_ref,
+    out_ref, new_ref,
+    q_buf, kv_buf, mixed, wbuf, bias, psend, precv, acc,
+    yx_s, yx_r, loc, ha_s, ha_r, wz_s, wz_r, wx_s, wx_r, wc_s, wc_r, pa_s, pa_r,
+):
+    T = qkv_ref.shape[0]
+    Dm = resid_ref.shape[1]
+    cw = Dm // S
+    hd = Dm // HEADS
+    hp = cw // hd
+    R = S // PAIR
+    G = F // PAIR
+    C = Dm // F
+    nk = (2 * H + 1) * T
+    f = lax.axis_index("fsdp")
+    s = lax.axis_index("seq")
+    z, y = lax.div(s, PAIR), lax.rem(s, PAIR)
+    g, c = lax.div(f, PAIR), lax.rem(f, PAIR)
+    partner = (f, z * PAIR + 1 - y)
+    twin = (g * PAIR + 1 - c, s)
+
+    def line(k):
+        return (f, lax.rem(z + k, R) * PAIR + y)
+
+    def across(k):
+        return (lax.rem(g + k, G) * PAIR + c, s)
+
+    barrier = pltpu.get_barrier_semaphore()
+    peers = [partner, twin] + [line(k) for k in range(1, R)] + [across(k) for k in range(1, G)]
+    for peer in peers:
+        pl.semaphore_signal(barrier, inc=1, device_id=peer, device_id_type=pl.DeviceIdType.MESH)
+    pl.semaphore_wait(barrier, len(peers))
+
+    def remote(src, dst, send, recv, to):
+        return pltpu.make_async_remote_copy(
+            src_ref=src, dst_ref=dst, send_sem=send, recv_sem=recv,
+            device_id=to, device_id_type=pl.DeviceIdType.MESH,
+        )
+
+    def cols(comp, j, half):
+        return pl.ds(pl.multiple_of(comp * Dm + (PAIR * j + half) * cw, cw), cw)
+
+    def place(comp, j, block):
+        if comp == 0:
+            return q_buf.at[j, pl.ds(pl.multiple_of(block * T, T), T), :]
+        return kv_buf.at[j, comp - 1, pl.ds(pl.multiple_of((H + block) * T, T), T), :]
+
+    def exchange(comp, j):
+        return remote(
+            qkv_ref.at[:, cols(comp, j, 1 - y)], place(comp, j, y),
+            yx_s.at[comp, j], yx_r.at[comp, j], partner,
+        )
+
+    def arrived(comp, j):
+        return remote(
+            qkv_ref.at[:, cols(comp, j, 1 - y)], place(comp, j, 1 - y),
+            yx_s.at[comp, j], yx_r.at[comp, j], partner,
+        )
+
+    def local(comp, j):
+        return pltpu.make_async_copy(
+            qkv_ref.at[:, cols(comp, j, y)], place(comp, j, y), loc.at[comp, j]
+        )
+
+    def halo(d, i, j):
+        b, slot = (2 - H + i, i) if d == 0 else (i, H + 2 + i)
+        to = (f, s + PAIR if d == 0 else s - PAIR)
+        return remote(
+            kv_buf.at[j, :, (H + b) * T : (H + b + 1) * T, :],
+            kv_buf.at[j, :, slot * T : (slot + 1) * T, :],
+            ha_s.at[d, i, j], ha_r.at[d, i, j], to,
+        )
+
+    sends = (z < R - 1, z > 0)
+    comes = (z > 0, z < R - 1)
+
+    def start_halos(j, own):
+        for d in range(2):
+            for i in range(H):
+                b = 2 - H + i if d == 0 else i
+                mine = (y == b) if own else (y != b)
+
+                @pl.when(jnp.logical_and(mine, sends[d]))
+                def _():
+                    halo(d, i, j).start()
+
+    def w_from(k):
+        return lax.rem(z + R - k, R)
+
+    def w_line(k):
+        return remote(wbuf.at[f, z], wbuf.at[f, z], wz_s.at[k], wz_r.at[k], line(k))
+
+    def w_line_in(k):
+        at = wbuf.at[f, w_from(k)]
+        return remote(at, at, wz_s.at[k], wz_r.at[k], line(k))
+
+    def w_across(k, n):
+        at = wbuf.at[f, w_from(k)]
+        return remote(at, at, wx_s.at[k, n], wx_r.at[k, n], across(n))
+
+    def w_across_in(k, n):
+        at = wbuf.at[lax.rem(g + G - n, G) * PAIR + c, w_from(k)]
+        return remote(at, at, wx_s.at[k, n], wx_r.at[k, n], across(n))
+
+    def w_twin(k, n):
+        at = wbuf.at[lax.rem(g + G - n, G) * PAIR + c, w_from(k)]
+        return remote(at, at, wc_s.at[k, n], wc_r.at[k, n], twin)
+
+    def w_twin_in(k, n):
+        at = wbuf.at[lax.rem(g + G - n, G) * PAIR + 1 - c, w_from(k)]
+        return remote(at, at, wc_s.at[k, n], wc_r.at[k, n], twin)
+
+    for j in range(R):
+        for comp in (1, 2):
+            exchange(comp, j).start()
+            local(comp, j).start()
+    for j in range(R):
+        exchange(0, j).start()
+        local(0, j).start()
+
+    new = (
+        ema_decay * tea_ref[...].astype(jnp.float32)
+        + (1.0 - ema_decay) * stu_ref[...].astype(jnp.float32)
+    ).astype(jnp.bfloat16)
+    new_ref[...] = new
+    wbuf[f, z] = new
+    for j in range(R):
+        local(1, j).wait()
+        local(2, j).wait()
+        start_halos(j, True)
+    for k in range(1, R):
+        w_line(k).start()
+
+    @pl.when(z == 0)
+    def _():
+        kv_buf[:, :, 0 : H * T, :] = jnp.zeros((R, 2, H * T, cw), jnp.bfloat16)
+
+    @pl.when(z == R - 1)
+    def _():
+        kv_buf[:, :, (H + 2) * T :, :] = jnp.zeros((R, 2, H * T, cw), jnp.bfloat16)
+
+    for b in range(2):
+        first = z * (PAIR * T) + b * T
+        rows = first + lax.broadcasted_iota(jnp.int32, (T, nk), 0)
+        keys = first - H * T + lax.broadcasted_iota(jnp.int32, (T, nk), 1)
+        row_segment = jnp.zeros((T, nk), jnp.int32)
+        key_segment = jnp.where(jnp.logical_or(keys < 0, keys >= S * T), -1, 0)
+        end = 0
+        for n in range(len_ref.shape[1]):
+            end = end + len_ref[0, n]
+            row_segment = row_segment + (rows >= end).astype(jnp.int32)
+            key_segment = key_segment + (keys >= end).astype(jnp.int32)
+        outside = jnp.logical_or(keys < 0, keys >= S * T)
+        same = jnp.logical_and(row_segment == key_segment, jnp.logical_not(outside))
+        bias[b] = jnp.where(same, 0.0, masked_score)
+
+    def forward(j, carry):
+        arrived(1, j).wait_recv()
+        arrived(2, j).wait_recv()
+        start_halos(j, False)
+        return carry
+
+    lax.fori_loop(0, R, forward, 0)
+
+    scale = log2_e / math.sqrt(hd)
+
+    def attend(j, carry):
+        @pl.when(j > 0)
+        def _():
+            w_line_in(j).wait_recv()
+
+        for n in range(1, G):
+            w_across(j, n).start()
+        w_twin(j, 0).start()
+
+        @pl.when(j > 0)
+        def _():
+            for n in range(1, G):
+                w_across_in(j - 1, n).wait_recv()
+                w_twin(j - 1, n).start()
+
+        local(0, j).wait()
+        arrived(0, j).wait_recv()
+        for d in range(2):
+            for i in range(H):
+
+                @pl.when(comes[d])
+                def _():
+                    halo(d, i, j).wait_recv()
+
+        head_of = lax.broadcasted_iota(jnp.int32, (T, cw), 1) // hd
+        for b in range(2):
+            query = q_buf[j, b * T : (b + 1) * T, :].astype(jnp.float32)
+            key = kv_buf[j, 0, b * T : b * T + nk, :]
+            value = kv_buf[j, 1, b * T : b * T + nk, :]
+            stacked = jnp.concatenate(
+                [jnp.where(head_of == h, query, 0.0).astype(jnp.bfloat16) for h in range(hp)], axis=0
+            )
+            scores = lax.dot_general(
+                stacked, key, (((1,), (1,)), ((), ())), preferred_element_type=jnp.float32
+            )
+            scores = scores.reshape(hp, T, nk) * scale + bias[b][None]
+            weights = jnp.exp2(scores - jnp.max(scores, axis=2, keepdims=True))
+            total = jnp.sum(weights, axis=2, keepdims=True)
+            summed = jnp.dot(
+                weights.astype(jnp.bfloat16).reshape(hp * T, nk), value,
+                preferred_element_type=jnp.float32,
+            ).reshape(hp, T, cw) / total
+            picked = summed[0]
+            for h in range(1, hp):
+                picked = jnp.where(head_of == h, summed[h], picked)
+            mixed[j, b * T : (b + 1) * T, :] = picked.astype(jnp.bfloat16)
+        return carry
+
+    lax.fori_loop(0, R, attend, 0)
+
+    for n in range(1, G):
+        w_across_in(R - 1, n).wait_recv()
+        w_twin(R - 1, n).start()
+
+    def w_done(k, carry):
+        for n in range(G):
+            w_twin_in(k, n).wait_recv()
+        return carry
+
+    lax.fori_loop(0, R, w_done, 0)
+
+    def part(block, col):
+        total = jnp.zeros((T, C), jnp.float32)
+        for j in range(R):
+            total = total + jnp.dot(
+                mixed[j, pl.ds(pl.multiple_of(block * T, T), T), :], wbuf[col, j],
+                preferred_element_type=jnp.float32,
+            )
+        return total
+
+    def give(col):
+        return remote(psend.at[col], precv.at[col], pa_s.at[col], pa_r.at[col], partner)
+
+    def give_part(col, carry):
+        psend[col] = part(1 - y, col).astype(jnp.bfloat16)
+        give(col).start()
+        return carry
+
+    def keep_part(col, carry):
+        acc[col] = part(y, col)
+        return carry
+
+    lax.fori_loop(0, F, give_part, 0)
+    lax.fori_loop(0, F, keep_part, 0)
+
+    total = jnp.zeros((T, 1), jnp.float32)
+    for col in range(F):
+        give(col).wait_recv()
+        branch = (acc[col] + precv[col].astype(jnp.float32)) * (1.0 / math.sqrt(Dm))
+        summed = resid_ref[:, col * C : (col + 1) * C].astype(jnp.float32) + branch
+        acc[col] = summed
+        total = total + jnp.sum(summed, axis=1, keepdims=True)
+    mean = total / Dm
+    square = jnp.zeros((T, 1), jnp.float32)
+    for col in range(F):
+        centered = acc[col] - mean
+        square = square + jnp.sum(centered * centered, axis=1, keepdims=True)
+    gain = lax.rsqrt(square / Dm + norm_epsilon)
+    for col in range(F):
+        at = slice(col * C, (col + 1) * C)
+        out_ref[:, at] = (earlier_ref[:, at] + (acc[col] - mean) * gain) * (1.0 / TOP_K)
+
+    def drain(j, carry):
+        for comp in range(3):
+            exchange(comp, j).wait_send()
+        for d in range(2):
+            for i in range(H):
+
+                @pl.when(sends[d])
+                def _():
+                    halo(d, i, j).wait_send()
+
+        @pl.when(j > 0)
+        def _():
+            w_line(j).wait_send()
+
+        for n in range(1, G):
+            w_across(j, n).wait_send()
+        for n in range(G):
+            w_twin(j, n).wait_send()
+        return carry
+
+    lax.fori_loop(0, R, drain, 0)
+
+    def drain_parts(col, carry):
+        give(col).wait_send()
+        return carry
+
+    lax.fori_loop(0, F, drain_parts, 0)
 
 
 def segment_ids(utt_lengths, frames):
-    utt_ends = jnp.cumsum(utt_lengths)
+    order = jnp.arange(utt_lengths.shape[0])
+    utt_ends = jnp.sum(jnp.where(order[None, :] <= order[:, None], utt_lengths[None, :], 0), axis=1)
     places = jnp.arange(frames, dtype=jnp.int32)
     return jnp.sum((places[:, None] >= utt_ends[None, :]).astype(jnp.int32), axis=1)
 
@@ -63,7 +366,7 @@
     return outputs.reshape(frames, stacked.shape[2], stacked.shape[3])
 
 
-def shards(qkv, resid, earlier, lengths, teacher_out, student_out):
+def spread(qkv, resid, earlier, lengths, teacher_out, student_out):
     teacher_new = (
         ema_decay * teacher_out.astype(jnp.float32)
         + (1.0 - ema_decay) * student_out.astype(jnp.float32)
@@ -77,14 +380,14 @@
         lax.all_to_all(own_heads, "seq", split_axis=2, concat_axis=0, tiled=True)[:, :, 0], segment
     )
     regathered = lax.all_to_all(attended[:, None], "seq", split_axis=0, concat_axis=1, tiled=True)
-    mixed_rows = regathered.reshape(tokens, D)
+    mixed_rows = regathered.reshape(tokens, HEADS * HEAD_DIM)
     full_rows = lax.all_gather(teacher_new, "seq", axis=0, tiled=True)
     branch = jnp.dot(
         mixed_rows,
         lax.all_gather(full_rows, "fsdp", axis=1, tiled=True),
         preferred_element_type=jnp.float32,
     )
-    branch = branch / math.sqrt(D)
+    branch = branch / math.sqrt(HEADS * HEAD_DIM)
     summed = resid[0].astype(jnp.float32) + branch
     centered = summed - jnp.mean(summed, axis=1, keepdims=True)
     normed = centered * lax.rsqrt(
@@ -92,6 +395,52 @@
     )
     targets = ((earlier[0] + normed) / TOP_K)[None]
     return (targets, teacher_new)
+
+
+def shards(F, S, qkv, resid, earlier, lengths, teacher_out, student_out):
+    T, width = qkv.shape[1:]
+    Dm = resid.shape[2]
+    longest = T * S // 8
+    H = -(-(longest - 1) // T)
+    R, G, C, cw = S // PAIR, F // PAIR, Dm // F, Dm // S
+    if S % PAIR or F % PAIR or H > PAIR or cw % 128 or C % 128 or T % 16:
+        return spread(qkv, resid, earlier, lengths, teacher_out, student_out)
+    nk = (2 * H + 1) * T
+    vmem = pl.BlockSpec(memory_space=pltpu.VMEM)
+    dma = pltpu.SemaphoreType.DMA
+    targets, teacher_new = pl.pallas_call(
+        functools.partial(body, F, S, H),
+        out_shape=(
+            jax.ShapeDtypeStruct((T, Dm), jnp.float32),
+            jax.ShapeDtypeStruct(teacher_out.shape, jnp.bfloat16),
+        ),
+        in_specs=[pl.BlockSpec(memory_space=pltpu.SMEM)] + [vmem] * 5,
+        out_specs=(vmem, vmem),
+        scratch_shapes=[
+            pltpu.VMEM((R, PAIR * T, cw), jnp.bfloat16),
+            pltpu.VMEM((R, 2, (PAIR + 2 * H) * T, cw), jnp.bfloat16),
+            pltpu.VMEM((R, PAIR * T, cw), jnp.bfloat16),
+            pltpu.VMEM((F, R) + teacher_out.shape, jnp.bfloat16),
+            pltpu.VMEM((PAIR, T, nk), jnp.float32),
+            pltpu.VMEM((F, T, C), jnp.bfloat16),
+            pltpu.VMEM((F, T, C), jnp.bfloat16),
+            pltpu.VMEM((F, T, C), jnp.float32),
+            dma((3, R)), dma((3, R)), dma((3, R)),
+            dma((2, H, R)), dma((2, H, R)),
+            dma((R,)), dma((R,)),
+            dma((R, G)), dma((R, G)),
+            dma((R, G)), dma((R, G)),
+            dma((F,)), dma((F,)),
+        ],
+        compiler_params=pltpu.CompilerParams(
+            collective_id=0, has_side_effects=True, vmem_limit_bytes=48 * 2**20
+        ),
+        cost_estimate=pl.CostEstimate(
+            flops=4 * T * nk * Dm + 2 * T * Dm * Dm, bytes_accessed=2 * T * width + 14 * T * Dm,
+            transcendentals=HEADS * T * nk,
+        ),
+    )(lengths, qkv[0], resid[0], earlier[0], teacher_out, student_out)
+    return (targets[None], teacher_new)
 
 
 def solution(mesh):
@@ -104,7 +453,7 @@
         P("seq", "fsdp"),
     )
     return jax.shard_map(
-        shards,
+        functools.partial(shards, mesh.shape["fsdp"], mesh.shape["seq"]),
         mesh=mesh,
         in_specs=placed,
         out_specs=(P("fsdp", "seq", None), P("seq", "fsdp")),

time: 166 us -> 75.4 us (0.45)
  the two profiles are of different devices: /device:TPU:0 before, /device:TPU:24 now
where the time goes in v1:
time: 75.4 us; the launch traced here: 74.3 us
  Pallas kernels  65.7 us (87%)
  local copies, waits for them, and re-layouts  7.89 us (10%)
    pallas_call x1, Pallas kernels, shards(): pl.pallas_call(functools.partial(body, F, S, H), out_shape=(jax.ShapeDtyp...  65.7 us
    unnamed x14, local copies, waits for them, and re-layouts  7.89 us

profile of v1, /device:TPU:24, one launch (start us, length us, event | category | flops | bytes accessed | tf_op | source)
XLA Modules:
  0.0 74.3 jit_solution(14620634992860458312)
XLA Ops:
  0.6 0.0 copy-start
  0.6 1.4 %copy-done = bf16[1,128,6144]{2,1,0:T(8,128)(2,1)S(1)} copy-done((bf16[1,128,6144]{2,1,0:T(8,128)(2,1)S(1)}, bf16[1,128,6144]{2,1,0:T(8,128)(2,1)}, u32[]{:S(2)}) %copy-start) | copy-done | bytes 1572888
  2.0 0.0 copy-start.1
  2.0 1.2 %copy-done.1 = f32[1,128,2048]{2,1,0:T(8,128)S(1)} copy-done((f32[1,128,2048]{2,1,0:T(8,128)S(1)}, f32[1,128,2048]{2,1,0:T(8,128)}, u32[]{:S(2)}) %copy-start.1) | copy-done | bytes 1048600
  3.3 0.0 copy-start.2
  3.3 1.0 %copy-done.2 = bf16[1,128,2048]{2,1,0:T(8,128)(2,1)S(1)} copy-done((bf16[1,128,2048]{2,1,0:T(8,128)(2,1)S(1)}, bf16[1,128,2048]{2,1,0:T(8,128)(2,1)}, u32[]{:S(2)}) %copy-start.2) | copy-done | bytes 524312
  4.3 0.0 copy-start.3
  4.3 0.9 %copy-done.3 = bf16[256,512]{1,0:T(8,128)(2,1)S(1)} copy-done((bf16[256,512]{1,0:T(8,128)(2,1)S(1)}, bf16[256,512]{1,0:T(8,128)(2,1)}, u32[]{:S(2)}) %copy-start.3) | copy-done | bytes 262168
  5.3 0.0 copy-start.4
  5.3 0.9 %copy-done.4 = bf16[256,512]{1,0:T(8,128)(2,1)S(1)} copy-done((bf16[256,512]{1,0:T(8,128)(2,1)S(1)}, bf16[256,512]{1,0:T(8,128)(2,1)}, u32[]{:S(2)}) %copy-start.4) | copy-done | bytes 262168
  6.2 0.0 copy-start.5
  6.2 0.7 copy-done.5
  6.9 65.7 %shard_map.77 = (f32[128,2048]{1,0:T(8,128)S(1)}, bf16[256,512]{1,0:T(8,128)(2,1)S(1)}) custom-call(s32[1,12]{1,0:T(1,128)S(1)} %copy-done.5, bf16[128,6144]{1,0:T(8,128)(2,1)S(1)} %bitcast.5, bf16[128,2048]{1,0:T(8,128)(2,1)S(1)} %bitcast.7, f32[128,2048]{1,0:T(8,128)S(1)} %bitcast.6, bf16[256,512]{1,0:T(8,128)(2,1)S(1)} %copy-done.3, ...), custom_call_target="tpu_custom_call" | custom-call | flops 1476395008 | bytes 5242880 | tf_op jit(solution)/shard_map/pallas_call | solution.py:411
  72.6 1.0 %copy.10 = f32[1,128,2048]{2,1,0:T(8,128)} copy(f32[1,128,2048]{2,1,0:T(8,128)S(1)} %bitcast.4) | data formatting | bytes 2097152
  73.6 0.7 copy.11
Async XLA Ops:
  0.6 1.4 %copy-start = (bf16[1,128,6144]{2,1,0:T(8,128)(2,1)S(1)}, bf16[1,128,6144]{2,1,0:T(8,128)(2,1)}, u32[]{:S(2)}) copy-start(bf16[1,128,6144]{2,1,0:T(8,128)(2,1)} %param.6) | copy-start | bytes 4718596
  2.0 1.2 %copy-start.1 = (f32[1,128,2048]{2,1,0:T(8,128)S(1)}, f32[1,128,2048]{2,1,0:T(8,128)}, u32[]{:S(2)}) copy-start(f32[1,128,2048]{2,1,0:T(8,128)} %param.8) | copy-start | bytes 3145732
  3.3 1.0 %copy-start.2 = (bf16[1,128,2048]{2,1,0:T(8,128)(2,1)S(1)}, bf16[1,128,2048]{2,1,0:T(8,128)(2,1)}, u32[]{:S(2)}) copy-start(bf16[1,128,2048]{2,1,0:T(8,128)(2,1)} %param.7) | copy-start | bytes 1572868
  4.3 0.9 %copy-start.3 = (bf16[256,512]{1,0:T(8,128)(2,1)S(1)}, bf16[256,512]{1,0:T(8,128)(2,1)}, u32[]{:S(2)}) copy-start(bf16[256,512]{1,0:T(8,128)(2,1)} %tea_ref.1) | copy-start | bytes 786436
  5.3 0.9 %copy-start.4 = (bf16[256,512]{1,0:T(8,128)(2,1)S(1)}, bf16[256,512]{1,0:T(8,128)(2,1)}, u32[]{:S(2)}) copy-start(bf16[256,512]{1,0:T(8,128)(2,1)} %stu_ref.1) | copy-start | bytes 786436
  6.2 0.7 copy-start.5

commit v2 on v1

--- a/solution.py
+++ b/solution.py
@@ -21,13 +21,14 @@
 
 def body(
     F, S, H,
-    len_ref, qkv_ref, resid_ref, earlier_ref, tea_ref, stu_ref,
+    len_ref, qkv_ref, resid_hbm, earlier_hbm, tea_hbm, stu_hbm,
     out_ref, new_ref,
+    resid_ref, earlier_ref, tea_ref, stu_ref, in_sem,
     q_buf, kv_buf, mixed, wbuf, bias, psend, precv, acc,
     yx_s, yx_r, loc, ha_s, ha_r, wz_s, wz_r, wx_s, wx_r, wc_s, wc_r, pa_s, pa_r,
 ):
     T = qkv_ref.shape[0]
-    Dm = resid_ref.shape[1]
+    Dm = resid_hbm.shape[1]
     cw = Dm // S
     hd = Dm // HEADS
     hp = cw // hd
@@ -48,6 +49,33 @@
     def across(k):
         return (lax.rem(g + k, G) * PAIR + c, s)
 
+    def cols(comp, j, half):
+        return pl.ds(pl.multiple_of(comp * Dm + (PAIR * j + half) * cw, cw), cw)
+
+    def place(comp, j, block):
+        if comp == 0:
+            return q_buf.at[j, pl.ds(pl.multiple_of(block * T, T), T), :]
+        return kv_buf.at[j, comp - 1, pl.ds(pl.multiple_of((H + block) * T, T), T), :]
+
+    def local(comp, j):
+        return pltpu.make_async_copy(
+            qkv_ref.at[:, cols(comp, j, y)], place(comp, j, y), loc.at[comp, j]
+        )
+
+    staged = [
+        pltpu.make_async_copy(src, dst, in_sem.at[n])
+        for n, (src, dst) in enumerate(
+            ((tea_hbm, tea_ref), (stu_hbm, stu_ref), (resid_hbm, resid_ref), (earlier_hbm, earlier_ref))
+        )
+    ]
+    for j in range(R):
+        local(1, j).start()
+        local(2, j).start()
+    staged[0].start()
+    staged[1].start()
+    for j in range(R):
+        local(0, j).start()
+
     barrier = pltpu.get_barrier_semaphore()
     peers = [partner, twin] + [line(k) for k in range(1, R)] + [across(k) for k in range(1, G)]
     for peer in peers:
@@ -60,14 +88,6 @@
             device_id=to, device_id_type=pl.DeviceIdType.MESH,
         )
 
-    def cols(comp, j, half):
-        return pl.ds(pl.multiple_of(comp * Dm + (PAIR * j + half) * cw, cw), cw)
-
-    def place(comp, j, block):
-        if comp == 0:
-            return q_buf.at[j, pl.ds(pl.multiple_of(block * T, T), T), :]
-        return kv_buf.at[j, comp - 1, pl.ds(pl.multiple_of((H + block) * T, T), T), :]
-
     def exchange(comp, j):
         return remote(
             qkv_ref.at[:, cols(comp, j, 1 - y)], place(comp, j, y),
@@ -78,11 +98,6 @@
         return remote(
             qkv_ref.at[:, cols(comp, j, 1 - y)], place(comp, j, 1 - y),
             yx_s.at[comp, j], yx_r.at[comp, j], partner,
-        )
-
-    def local(comp, j):
-        return pltpu.make_async_copy(
-            qkv_ref.at[:, cols(comp, j, y)], place(comp, j, y), loc.at[comp, j]
         )
 
     def halo(d, i, j):
@@ -134,25 +149,32 @@
         return remote(at, at, wc_s.at[k, n], wc_r.at[k, n], twin)
 
     for j in range(R):
-        for comp in (1, 2):
-            exchange(comp, j).start()
-            local(comp, j).start()
+        exchange(1, j).start()
+        exchange(2, j).start()
+        if j > 0:
+            exchange(0, j - 1).start()
+    exchange(0, R - 1).start()
+
     for j in range(R):
-        exchange(0, j).start()
-        local(0, j).start()
-
+        local(1, j).wait()
+        local(2, j).wait()
+        start_halos(j, True)
+
+    staged[0].wait()
+    staged[1].wait()
     new = (
         ema_decay * tea_ref[...].astype(jnp.float32)
         + (1.0 - ema_decay) * stu_ref[...].astype(jnp.float32)
     ).astype(jnp.bfloat16)
     new_ref[...] = new
     wbuf[f, z] = new
-    for j in range(R):
-        local(1, j).wait()
-        local(2, j).wait()
-        start_halos(j, True)
+    for n in range(1, G):
+        w_across(0, n).start()
+    w_twin(0, 0).start()
     for k in range(1, R):
         w_line(k).start()
+    staged[2].start()
+    staged[3].start()
 
     @pl.when(z == 0)
     def _():
@@ -177,24 +199,23 @@
         same = jnp.logical_and(row_segment == key_segment, jnp.logical_not(outside))
         bias[b] = jnp.where(same, 0.0, masked_score)
 
-    def forward(j, carry):
+    def forward(j):
         arrived(1, j).wait_recv()
         arrived(2, j).wait_recv()
         start_halos(j, False)
-        return carry
-
-    lax.fori_loop(0, R, forward, 0)
+
+    forward(0)
 
     scale = log2_e / math.sqrt(hd)
 
     def attend(j, carry):
-        @pl.when(j > 0)
+        @pl.when(j < R - 1)
         def _():
-            w_line_in(j).wait_recv()
-
-        for n in range(1, G):
-            w_across(j, n).start()
-        w_twin(j, 0).start()
+            forward(j + 1)
+            w_line_in(j + 1).wait_recv()
+            for n in range(1, G):
+                w_across(j + 1, n).start()
+            w_twin(j + 1, 0).start()
 
         @pl.when(j > 0)
         def _():
@@ -237,17 +258,6 @@
 
     lax.fori_loop(0, R, attend, 0)
 
-    for n in range(1, G):
-        w_across_in(R - 1, n).wait_recv()
-        w_twin(R - 1, n).start()
-
-    def w_done(k, carry):
-        for n in range(G):
-            w_twin_in(k, n).wait_recv()
-        return carry
-
-    lax.fori_loop(0, R, w_done, 0)
-
     def part(block, col):
         total = jnp.zeros((T, C), jnp.float32)
         for j in range(R):
@@ -260,18 +270,32 @@
     def give(col):
         return remote(psend.at[col], precv.at[col], pa_s.at[col], pa_r.at[col], partner)
 
-    def give_part(col, carry):
+    def give_part(col):
         psend[col] = part(1 - y, col).astype(jnp.bfloat16)
         give(col).start()
-        return carry
+
+    def twin_part(n):
+        for k in range(R):
+            w_twin_in(k, n).wait_recv()
+        give_part(lax.rem(g + G - n, G) * PAIR + 1 - c)
+
+    give_part(f)
+    twin_part(0)
+    for n in range(1, G):
+        w_across_in(R - 1, n).wait_recv()
+        w_twin(R - 1, n).start()
+        give_part(lax.rem(g + G - n, G) * PAIR + c)
+    for n in range(1, G):
+        twin_part(n)
 
     def keep_part(col, carry):
         acc[col] = part(y, col)
         return carry
 
-    lax.fori_loop(0, F, give_part, 0)
     lax.fori_loop(0, F, keep_part, 0)
 
+    staged[2].wait()
+    staged[3].wait()
     total = jnp.zeros((T, 1), jnp.float32)
     for col in range(F):
         give(col).wait_recv()
@@ -407,6 +431,7 @@
         return spread(qkv, resid, earlier, lengths, teacher_out, student_out)
     nk = (2 * H + 1) * T
     vmem = pl.BlockSpec(memory_space=pltpu.VMEM)
+    hbm = pl.BlockSpec(memory_space=pltpu.HBM)
     dma = pltpu.SemaphoreType.DMA
     targets, teacher_new = pl.pallas_call(
         functools.partial(body, F, S, H),
@@ -414,9 +439,14 @@
             jax.ShapeDtypeStruct((T, Dm), jnp.float32),
             jax.ShapeDtypeStruct(teacher_out.shape, jnp.bfloat16),
         ),
-        in_specs=[pl.BlockSpec(memory_space=pltpu.SMEM)] + [vmem] * 5,
+        in_specs=[pl.BlockSpec(memory_space=pltpu.SMEM)] + [hbm] * 5,
         out_specs=(vmem, vmem),
         scratch_shapes=[
+            pltpu.VMEM((T, Dm), resid.dtype),
+            pltpu.VMEM((T, Dm), earlier.dtype),
+            pltpu.VMEM(teacher_out.shape, teacher_out.dtype),
+            pltpu.VMEM(student_out.shape, student_out.dtype),
+            dma((4,)),
             pltpu.VMEM((R, PAIR * T, cw), jnp.bfloat16),
             pltpu.VMEM((R, 2, (PAIR + 2 * H) * T, cw), jnp.bfloat16),
             pltpu.VMEM((R, PAIR * T, cw), jnp.bfloat16),
@@ -433,7 +463,7 @@
             dma((F,)), dma((F,)),
         ],
         compiler_params=pltpu.CompilerParams(
-            collective_id=0, has_side_effects=True, vmem_limit_bytes=48 * 2**20
+            collective_id=0, has_side_effects=True, vmem_limit_bytes=63 * 2**20
         ),
         cost_estimate=pl.CostEstimate(
             flops=4 * T * nk * Dm + 2 * T * Dm * Dm, bytes_accessed=2 * T * width + 14 * T * Dm,

time: 75.4 us -> 65.8 us (0.87); the launches traced: 74.3 us -> 65.7 us
  local copies, waits for them, and re-layouts: 7.89 us -> 3.04 us
  Pallas kernels: 65.7 us -> 62 us
    unnamed x14 -> x4, local copies, waits for them, and re-layouts: 7.89 us -> 3.04 us
    pallas_call x1, Pallas kernels: 65.7 us -> 62 us  [shards(): pl.pallas_call(functools.partial(body, F, S, H), out_shape=(jax.ShapeDtyp...]
where the time goes in v2:
time: 65.8 us; the launch traced here: 65.7 us
  Pallas kernels  62 us (94%)
  local copies, waits for them, and re-layouts  3.04 us (5%)
    pallas_call x1, Pallas kernels, shards(): pl.pallas_call(functools.partial(body, F, S, H), out_shape=(jax.ShapeDtyp...  62 us
    unnamed x4, local copies, waits for them, and re-layouts  3.04 us

profile of v2, /device:TPU:24, one launch (start us, length us, event | category | flops | bytes accessed | tf_op | source)
XLA Modules:
  0.0 65.7 jit_solution(9187629112892785500)
XLA Ops:
  0.6 62.0 %shard_map.77 = (f32[128,2048]{1,0:T(8,128)}, bf16[256,512]{1,0:T(8,128)(2,1)}) custom-call(s32[1,12]{1,0:T(1,128)} %len_ref.1, bf16[128,6144]{1,0:T(8,128)(2,1)} %bitcast.5, bf16[128,2048]{1,0:T(8,128)(2,1)} %bitcast.7, f32[128,2048]{1,0:T(8,128)} %bitcast.6, bf16[256,512]{1,0:T(8,128)(2,1)} %tea_hbm.1, bf16[256,512]{1,0:T(8,128)(2,1)} %stu_hbm.1), custom_call_target="tpu_custom_call" | custom-call | flops 1476395008 | bytes 5242880 | tf_op jit(solution)/shard_map/pallas_call | solution.py:436
  62.6 0.0 copy-start
  62.6 2.3 %copy.10 = f32[1,128,2048]{2,1,0:T(8,128)} copy(f32[1,128,2048]{2,1,0:T(8,128)} %bitcast.4) | data formatting | bytes 2097152
  65.0 0.0 copy-done
  65.0 0.7 %copy.11 = bf16[256,512]{1,0:T(8,128)(2,1)} copy(bf16[256,512]{1,0:T(8,128)(2,1)S(1)} %copy-done) | data formatting | bytes 524288
Async XLA Ops:
  62.6 2.4 %copy-start = (bf16[256,512]{1,0:T(8,128)(2,1)S(1)}, bf16[256,512]{1,0:T(8,128)(2,1)}, u32[]{:S(2)}) copy-start(bf16[256,512]{1,0:T(8,128)(2,1)} %get-tuple-element.9) | copy-start | bytes 786436

commit v3 on v2

--- a/solution.py
+++ b/solution.py
@@ -208,7 +208,7 @@
 
     scale = log2_e / math.sqrt(hd)
 
-    def attend(j, carry):
+    def gather(j):
         @pl.when(j < R - 1)
         def _():
             forward(j + 1)
@@ -232,31 +232,42 @@
                 def _():
                     halo(d, i, j).wait_recv()
 
-        head_of = lax.broadcasted_iota(jnp.int32, (T, cw), 1) // hd
-        for b in range(2):
-            query = q_buf[j, b * T : (b + 1) * T, :].astype(jnp.float32)
-            key = kv_buf[j, 0, b * T : b * T + nk, :]
-            value = kv_buf[j, 1, b * T : b * T + nk, :]
-            stacked = jnp.concatenate(
-                [jnp.where(head_of == h, query, 0.0).astype(jnp.bfloat16) for h in range(hp)], axis=0
-            )
-            scores = lax.dot_general(
-                stacked, key, (((1,), (1,)), ((), ())), preferred_element_type=jnp.float32
-            )
-            scores = scores.reshape(hp, T, nk) * scale + bias[b][None]
-            weights = jnp.exp2(scores - jnp.max(scores, axis=2, keepdims=True))
-            total = jnp.sum(weights, axis=2, keepdims=True)
-            summed = jnp.dot(
-                weights.astype(jnp.bfloat16).reshape(hp * T, nk), value,
-                preferred_element_type=jnp.float32,
-            ).reshape(hp, T, cw) / total
-            picked = summed[0]
-            for h in range(1, hp):
-                picked = jnp.where(head_of == h, summed[h], picked)
-            mixed[j, b * T : (b + 1) * T, :] = picked.astype(jnp.bfloat16)
+    head_of = lax.broadcasted_iota(jnp.int32, (T, cw), 1) // hd
+
+    def attend(j, b):
+        at = pl.ds(pl.multiple_of(b * T, T), T)
+        span = pl.ds(pl.multiple_of(b * T, T), nk)
+        query = q_buf[j, at, :].astype(jnp.float32)
+        stacked = jnp.concatenate(
+            [jnp.where(head_of == h, query, 0.0).astype(jnp.bfloat16) for h in range(hp)], axis=0
+        )
+        scores = lax.dot_general(
+            stacked, kv_buf[j, 0, span, :], (((1,), (1,)), ((), ())),
+            preferred_element_type=jnp.float32,
+        )
+        scores = scores.reshape(hp, T, nk) * scale + bias[b][None]
+        weights = jnp.exp2(scores - jnp.max(scores, axis=2, keepdims=True))
+        total = jnp.sum(weights, axis=2, keepdims=True)
+        summed = jnp.dot(
+            weights.astype(jnp.bfloat16).reshape(hp * T, nk), kv_buf[j, 1, span, :],
+            preferred_element_type=jnp.float32,
+        ).reshape(hp, T, cw)
+        picked, below = summed[0], total[0]
+        for h in range(1, hp):
+            picked = jnp.where(head_of == h, summed[h], picked)
+            below = jnp.where(head_of == h, total[h], below)
+        mixed[j, at, :] = (picked / below).astype(jnp.bfloat16)
+
+    def attend_partner(j, carry):
+        gather(j)
+        attend(j, 1 - y)
         return carry
 
-    lax.fori_loop(0, R, attend, 0)
+    def attend_own(j, carry):
+        attend(j, y)
+        return carry
+
+    lax.fori_loop(0, R, attend_partner, 0)
 
     def part(block, col):
         total = jnp.zeros((T, C), jnp.float32)
@@ -284,6 +295,8 @@
     for n in range(1, G):
         w_across_in(R - 1, n).wait_recv()
         w_twin(R - 1, n).start()
+    lax.fori_loop(0, R, attend_own, 0)
+    for n in range(1, G):
         give_part(lax.rem(g + G - n, G) * PAIR + c)
     for n in range(1, G):
         twin_part(n)

time: 65.8 us -> 66.1 us (level)
  no operation moved by 1% of the time
where the time goes in v3:
time: 66.1 us; the launch traced here: 65.9 us
  Pallas kernels  62.2 us (94%)
  local copies, waits for them, and re-layouts  3.04 us (5%)
    pallas_call x1, Pallas kernels, shards(): pl.pallas_call(functools.partial(body, F, S, H), out_shape=(jax.ShapeDtyp...  62.2 us
    unnamed x4, local copies, waits for them, and re-layouts  3.04 us

profile of v3, /device:TPU:24, one launch (start us, length us, event | category | flops | bytes accessed | tf_op | source)
XLA Modules:
  0.0 65.9 jit_solution(8504291916318476063)
XLA Ops:
  0.6 62.2 %shard_map.77 = (f32[128,2048]{1,0:T(8,128)}, bf16[256,512]{1,0:T(8,128)(2,1)}) custom-call(s32[1,12]{1,0:T(1,128)} %len_ref.1, bf16[128,6144]{1,0:T(8,128)(2,1)} %bitcast.5, bf16[128,2048]{1,0:T(8,128)(2,1)} %bitcast.7, f32[128,2048]{1,0:T(8,128)} %bitcast.6, bf16[256,512]{1,0:T(8,128)(2,1)} %tea_hbm.1, bf16[256,512]{1,0:T(8,128)(2,1)} %stu_hbm.1), custom_call_target="tpu_custom_call" | custom-call | flops 1476395008 | bytes 5242880 | tf_op jit(solution)/shard_map/pallas_call | solution.py:449
  62.9 0.0 copy-start
  62.9 2.3 %copy.10 = f32[1,128,2048]{2,1,0:T(8,128)} copy(f32[1,128,2048]{2,1,0:T(8,128)} %bitcast.4) | data formatting | bytes 2097152
  65.2 0.0 copy-done
  65.2 0.7 %copy.11 = bf16[256,512]{1,0:T(8,128)(2,1)} copy(bf16[256,512]{1,0:T(8,128)(2,1)S(1)} %copy-done) | data formatting | bytes 524288
Async XLA Ops:
  62.9 2.4 %copy-start = (bf16[256,512]{1,0:T(8,128)(2,1)S(1)}, bf16[256,512]{1,0:T(8,128)(2,1)}, u32[]{:S(2)}) copy-start(bf16[256,512]{1,0:T(8,128)(2,1)} %get-tuple-element.9) | copy-start | bytes 786436

commit v4 on v2

--- a/solution.py
+++ b/solution.py
@@ -122,30 +122,66 @@
                 def _():
                     halo(d, i, j).start()
 
-    def w_from(k):
-        return lax.rem(z + R - k, R)
-
-    def w_line(k):
-        return remote(wbuf.at[f, z], wbuf.at[f, z], wz_s.at[k], wz_r.at[k], line(k))
-
-    def w_line_in(k):
-        at = wbuf.at[f, w_from(k)]
-        return remote(at, at, wz_s.at[k], wz_r.at[k], line(k))
+    def w_block(d, dist):
+        return z - dist if d == 0 else z + dist
+
+    def w_has(d, dist):
+        return z >= dist if d == 0 else z + dist < R
+
+    def w_pass(d, dist):
+        at = wbuf.at[f, w_block(d, dist)]
+        to = (f, s + PAIR if d == 0 else s - PAIR)
+        return remote(at, at, wz_s.at[d, dist], wz_r.at[d, dist], to)
+
+    def w_pass_in(d, dist):
+        at = wbuf.at[f, w_block(d, dist)]
+        to = (f, s + PAIR if d == 0 else s - PAIR)
+        return remote(at, at, wz_s.at[d, dist - 1], wz_r.at[d, dist - 1], to)
+
+    def w_spread(block):
+        for n in range(1, G):
+            w_across(block, n).start()
+        w_twin(block, 0).start()
+
+    def w_arrivals(dist):
+        for d in range(2):
+
+            @pl.when(w_has(d, dist))
+            def _():
+                w_pass_in(d, dist).wait_recv()
+
+                @pl.when(sends[d])
+                def _():
+                    w_pass(d, dist).start()
+
+                w_spread(w_block(d, dist))
+
+    def w_share(block):
+        for n in range(1, G):
+            w_across_in(block, n).wait_recv()
+            w_twin(block, n).start()
+
+    def w_shares(dist):
+        for d in range(2):
+
+            @pl.when(w_has(d, dist))
+            def _():
+                w_share(w_block(d, dist))
 
     def w_across(k, n):
-        at = wbuf.at[f, w_from(k)]
+        at = wbuf.at[f, k]
         return remote(at, at, wx_s.at[k, n], wx_r.at[k, n], across(n))
 
     def w_across_in(k, n):
-        at = wbuf.at[lax.rem(g + G - n, G) * PAIR + c, w_from(k)]
+        at = wbuf.at[lax.rem(g + G - n, G) * PAIR + c, k]
         return remote(at, at, wx_s.at[k, n], wx_r.at[k, n], across(n))
 
     def w_twin(k, n):
-        at = wbuf.at[lax.rem(g + G - n, G) * PAIR + c, w_from(k)]
+        at = wbuf.at[lax.rem(g + G - n, G) * PAIR + c, k]
         return remote(at, at, wc_s.at[k, n], wc_r.at[k, n], twin)
 
     def w_twin_in(k, n):
-        at = wbuf.at[lax.rem(g + G - n, G) * PAIR + 1 - c, w_from(k)]
+        at = wbuf.at[lax.rem(g + G - n, G) * PAIR + 1 - c, k]
         return remote(at, at, wc_s.at[k, n], wc_r.at[k, n], twin)
 
     for j in range(R):
@@ -168,11 +204,13 @@
     ).astype(jnp.bfloat16)
     new_ref[...] = new
     wbuf[f, z] = new
-    for n in range(1, G):
-        w_across(0, n).start()
-    w_twin(0, 0).start()
-    for k in range(1, R):
-        w_line(k).start()
+    for d in range(2):
+
+        @pl.when(sends[d])
+        def _():
+            w_pass(d, 0).start()
+
+    w_spread(z)
     staged[2].start()
     staged[3].start()
 
@@ -212,16 +250,15 @@
         @pl.when(j < R - 1)
         def _():
             forward(j + 1)
-            w_line_in(j + 1).wait_recv()
-            for n in range(1, G):
-                w_across(j + 1, n).start()
-            w_twin(j + 1, 0).start()
-
-        @pl.when(j > 0)
+            w_arrivals(j + 1)
+
+        @pl.when(j == 1)
         def _():
-            for n in range(1, G):
-                w_across_in(j - 1, n).wait_recv()
-                w_twin(j - 1, n).start()
+            w_share(z)
+
+        @pl.when(j > 1)
+        def _():
+            w_shares(j - 1)
 
         local(0, j).wait()
         arrived(0, j).wait_recv()
@@ -281,9 +318,11 @@
 
     give_part(f)
     twin_part(0)
+    if R > 1:
+        w_shares(R - 1)
+    else:
+        w_share(z)
     for n in range(1, G):
-        w_across_in(R - 1, n).wait_recv()
-        w_twin(R - 1, n).start()
         give_part(lax.rem(g + G - n, G) * PAIR + c)
     for n in range(1, G):
         twin_part(n)
@@ -323,9 +362,11 @@
                 def _():
                     halo(d, i, j).wait_send()
 
-        @pl.when(j > 0)
-        def _():
-            w_line(j).wait_send()
+        for d in range(2):
+
+            @pl.when(jnp.logical_and(w_has(d, j), sends[d]))
+            def _():
+                w_pass(d, j).wait_send()
 
         for n in range(1, G):
             w_across(j, n).wait_send()
@@ -457,7 +498,7 @@
             pltpu.VMEM((F, T, C), jnp.float32),
             dma((3, R)), dma((3, R)), dma((3, R)),
             dma((2, H, R)), dma((2, H, R)),
-            dma((R,)), dma((R,)),
+            dma((2, R)), dma((2, R)),
             dma((R, G)), dma((R, G)),
             dma((R, G)), dma((R, G)),
             dma((F,)), dma((F,)),

time: 65.8 us -> 61.6 us (0.936)
  the two profiles are of different devices: /device:TPU:24 before, /device:TPU:0 now
where the time goes in v4:
time: 61.6 us; the launch traced here: 61.4 us
  Pallas kernels  57.7 us (94%)
  local copies, waits for them, and re-layouts  3.04 us (5%)
  between operations  0.65 us (1%)
    pallas_call x1, Pallas kernels, shards(): pl.pallas_call(functools.partial(body, F, S, H), out_shape=(jax.ShapeDtyp...  57.7 us
    unnamed x4, local copies, waits for them, and re-layouts  3.04 us

profile of v4, /device:TPU:0, one launch (start us, length us, event | category | flops | bytes accessed | tf_op | source)
XLA Modules:
  0.0 61.4 jit_solution(10905298324327796829)
XLA Ops:
  0.6 57.7 %shard_map.77 = (f32[128,2048]{1,0:T(8,128)}, bf16[256,512]{1,0:T(8,128)(2,1)}) custom-call(s32[1,12]{1,0:T(1,128)} %len_ref.1, bf16[128,6144]{1,0:T(8,128)(2,1)} %bitcast.5, bf16[128,2048]{1,0:T(8,128)(2,1)} %bitcast.7, f32[128,2048]{1,0:T(8,128)} %bitcast.6, bf16[256,512]{1,0:T(8,128)(2,1)} %tea_hbm.1, bf16[256,512]{1,0:T(8,128)(2,1)} %stu_hbm.1), custom_call_target="tpu_custom_call" | custom-call | flops 1476395008 | bytes 5242880 | tf_op jit(solution)/shard_map/pallas_call | solution.py:477
  58.4 0.0 copy-start
  58.4 2.3 %copy.10 = f32[1,128,2048]{2,1,0:T(8,128)} copy(f32[1,128,2048]{2,1,0:T(8,128)} %bitcast.4) | data formatting | bytes 2097152
  60.7 0.0 copy-done
  60.7 0.7 %copy.11 = bf16[256,512]{1,0:T(8,128)(2,1)} copy(bf16[256,512]{1,0:T(8,128)(2,1)S(1)} %copy-done) | data formatting | bytes 524288
Async XLA Ops:
  58.4 2.4 %copy-start = (bf16[256,512]{1,0:T(8,128)(2,1)S(1)}, bf16[256,512]{1,0:T(8,128)(2,1)}, u32[]{:S(2)}) copy-start(bf16[256,512]{1,0:T(8,128)(2,1)} %get-tuple-element.9) | copy-start | bytes 786436
